TPU v7x, 256 devices: a whole 4x4x8 slice. The times are simulated.
256 devices in a mesh: band: 32 (over z, x_hi, core), fft: 8 (over x_lo, y).
Axes of the slice: x: 4 (x_hi: 2, x_lo: 2; x = x_hi * 2 + x_lo), y: 4, z: 8, core: 2. Of those that a mesh axis runs over, the one named last changes fastest.
Arguments:
- orbitals: float32 [64, 64, 4096], P('band', 'fft'), may hold values from -6 to 6
Outputs:
- local_exchange: float32 [64, 64, 4096], P('band', 'fft')
- window_exchange: float32 [4, 64, 4096], P(None, 'fft')
All inputs are finite; a program needn't handle non-finite values.
Results may differ from a plain program's by a relative error of at most 0.00019.
Values sent between devices are 32-bit elements; how exact they have to be, the bound alone decides.
A program may use at most 64 MiB of HBM per device.

v0:
```python
import math

import jax
import jax.numpy as jnp
from jax import lax
from jax.sharding import PartitionSpec as P

GRID = 64


spacing = 0.367
mixing = 0.25
highest = lax.Precision.HIGHEST


def broadcast(value, axis, root):
    mine = lax.axis_index(axis) == root
    return lax.psum(jnp.where(mine, value, jnp.zeros_like(value)), axis)


def folded(values, extent):
    return jnp.where(2 * values < extent, values, values - extent)


def coulomb(kx_index, ky_index, kz_index, extent):
    squared = (
        folded(kx_index, extent) ** 2
        + folded(ky_index, extent) ** 2
        + folded(kz_index, extent) ** 2
    )
    factor = (2.0 * math.pi / (extent * spacing)) ** 2
    clamped = jnp.maximum(squared, 1).astype(jnp.float32)
    return jnp.where(squared > 0, 4.0 * math.pi / factor / clamped, jnp.float32(0.0))


def make_tables(extent):
    counter = jnp.arange(extent, dtype=jnp.int32)
    phases = counter[:, None] * counter[None, :] % extent
    angles = phases.astype(jnp.float32) * (2.0 * math.pi / extent)
    cosine = jnp.cos(angles)
    sine_table = jnp.sin(angles)
    forward = jnp.concatenate(
        [jnp.concatenate([cosine, -sine_table], 1), jnp.concatenate([sine_table, cosine], 1)], 0
    )
    inverse = jnp.concatenate(
        [jnp.concatenate([cosine, sine_table], 1), jnp.concatenate([-sine_table, cosine], 1)], 0
    )
    return (cosine, sine_table, forward, inverse)


def along_axis(packed_field, pattern, cosine, sine_table, direction):
    cos_part = jnp.einsum(pattern, cosine, packed_field, precision=highest)
    sin_part = jnp.einsum(pattern, sine_table, packed_field, precision=highest)
    half_width = packed_field.shape[-1] // 2
    real_part = cos_part[..., :half_width] + direction * sin_part[..., half_width:]
    imag_part = cos_part[..., half_width:] - direction * sin_part[..., :half_width]
    return jnp.concatenate([real_part, imag_part], -1)


def along_depth(packed_field, matrix):
    return jnp.einsum("nxyc,cd->nxyd", packed_field, matrix, precision=highest)


def planes_potential(packed_field, tables_all, kernel):
    cosine, sine_table, forward, inverse = tables_all
    extent = cosine.shape[0]
    spectrum = along_axis(
        along_depth(packed_field, forward), "ky,nxyc->nxkc", cosine, sine_table, 1.0
    )
    pencils = lax.all_to_all(spectrum, "fft", split_axis=2, concat_axis=1, tiled=True)
    pencils = along_axis(pencils, "kx,nxyc->nkyc", cosine, sine_table, 1.0) * kernel
    pencils = along_axis(pencils, "kx,nxyc->nkyc", cosine, sine_table, -1.0)
    returned = lax.all_to_all(pencils, "fft", split_axis=1, concat_axis=2, tiled=True)
    returned = along_axis(returned, "ky,nxyc->nxkc", cosine, sine_table, -1.0)
    return along_depth(returned, inverse) * (1.0 / extent**3)


def block_sweep(orbitals, blocks, local_out, tables_all, kernel):
    own_count, planes, flat_width = orbitals.shape
    extent = tables_all[0].shape[0]
    block_width = blocks.shape[0]
    block_grid = blocks.reshape(block_width, planes, extent, extent)

    def advance(orbital_index, state):
        local_acc, window_acc = state
        own_orbital = lax.dynamic_slice_in_dim(orbitals, orbital_index, 1, 0).reshape(
            1, planes, extent, extent
        )
        density = own_orbital * block_grid
        packed_field = jnp.concatenate([density, jnp.zeros_like(density)], -1)
        potential = planes_potential(packed_field, tables_all, kernel)[..., :extent]
        exchange_term = -mixing * jnp.sum(block_grid * potential, 0, keepdims=True)
        current = lax.dynamic_slice_in_dim(local_acc, orbital_index, 1, 0)
        local_acc = lax.dynamic_update_slice_in_dim(
            local_acc, current + exchange_term, orbital_index, 0
        )
        window_acc = window_acc - mixing * own_orbital * potential
        return (local_acc, window_acc)

    return lax.fori_loop(0, own_count, advance, (local_out, jnp.zeros_like(block_grid)))


def body(orbitals):
    own_count, planes, flat_width = orbitals.shape
    extent = GRID
    band_count = lax.axis_size("band")
    tables_all = make_tables(extent)
    root_list = (0, band_count // 2)
    spans = jnp.arange(extent, dtype=jnp.int32)
    ky_global = lax.axis_index("fft") * planes + jnp.arange(planes, dtype=jnp.int32)
    pencil = coulomb(spans[:, None, None], ky_global[None, :, None], spans[None, None, :], extent)
    kernel = jnp.concatenate([pencil, pencil], -1)
    local_out = jnp.zeros((own_count, planes, extent, extent), jnp.float32)
    pieces = []
    for root in root_list:
        local_out, window_piece = block_sweep(
            orbitals, broadcast(orbitals, "band", root), local_out, tables_all, kernel
        )
        pieces.append(window_piece)
    window_part = jnp.concatenate(pieces, 0)
    window_total = lax.psum(window_part, "band")
    return (
        local_out.reshape(own_count, planes, extent * extent),
        window_total.reshape(window_total.shape[0], planes, extent * extent),
    )


def solution(mesh):
    return jax.shard_map(
        body,
        mesh=mesh,
        in_specs=(P("band", "fft", None),),
        out_specs=(P("band", "fft", None), P(None, "fft", None)),
        check_vma=False,
    )
```

profile of v0, /device:TPU:1, one launch (start us, length us, event | category | flops | bytes accessed | tf_op | source)
XLA Modules:
  0.0 711.1 jit_solution(3323559831417157062)
XLA Ops:
  7.2 1.0 broadcast_select_fusion
  8.2 1.0 reshape.148
  9.2 1.0 reshape.149
  11.2 273.9 %all-reduce.8.cloned.1.call-done = (f32[2,8,64,64]{3,2,1,0:T(8,128)}, f32[2,8,64,64]{3,2,1,0:T(8,128)}) async-done(((f32[2,8,64,64]{3,2,1,0:T(8,128)}, f32[2,8,64,64]{3,2,1,0:T(8,128)}), (f32[2,8,64,64]{3,2,1,0:T(8,128)}, f32[2,8,64,64]{3,2,1,0:T(8,128)})) %all-reduce.8.cloned.1.call-update) | async-done | bytes 524304 | tf_op jit(solution)/shard_map/psum | solution.py:18
  285.1 1.0 copy-done.1
  286.1 70.4 %while.34 = (s32[]{:T(128)}, f32[2,8,64,64]{3,2,1,0:T(8,128)S(1)}, f32[2,8,64,64]{3,2,1,0:T(8,128)}, f32[2,8,4096]{2,1,0:T(8,128)}, f32[2,8,64,64]{3,2,1,0:T(8,1...) while((s32[]{:T(128)}, f32[2,8,64,64]{3,2,1,0:T(8,128)S(1)}, ...), condition=%wide.region_3.4_spmd.clone.clone, body=%wide.region_1.3_spmd.clone.clone.sunk | while | flops 1210646528 | bytes 29622484 | solution.py:100
  286.1 1.0 constant_dynamic-slice_fusion.4
  290.2 12.5 %all_to_all.160 = f32[2,8,64,128]{3,1,0,2:T(8,128)S(1)} all-to-all(f32[2,8,64,128]{3,1,0,2:T(8,128)S(1)} %copy.71), channel_id=1, replica_groups=mesh['band'=32,'fft'=8] {'fft'}, dimensions={2} | all-to-all | bytes 1048576 | tf_op jit(solution)/shard_map/while/body/eval_jaxpr/all_to_all | solution.py:70
  302.7 0.7 convolution_bitcast_fusion.34
  304.5 0.8 convolution_bitcast_fusion.37
  305.3 0.8 convolution_bitcast_fusion.36
  306.7 1.1 copy.72
  307.8 3.5 all-to-all-start.1
  311.4 7.0 all-to-all-done.1
  322.3 0.9 constant_dynamic-slice_fusion.4
  324.0 0.7 convolution_bitcast_fusion.32
  326.3 10.5 %all_to_all.160 = f32[2,8,64,128]{3,1,0,2:T(8,128)S(1)} all-to-all(f32[2,8,64,128]{3,1,0,2:T(8,128)S(1)} %copy.71), channel_id=1, replica_groups=mesh['band'=32,'fft'=8] {'fft'}, dimensions={2} | all-to-all | bytes 1048576 | tf_op jit(solution)/shard_map/while/body/eval_jaxpr/all_to_all | solution.py:70
  336.9 0.7 convolution_bitcast_fusion.34
  338.7 0.8 convolution_bitcast_fusion.37
  339.5 0.8 convolution_bitcast_fusion.36
  340.9 1.1 copy.72
  342.0 3.5 all-to-all-start.1
  345.5 7.0 all-to-all-done.1
  356.5 65.3 %while.35 = (s32[]{:T(128)}, f32[2,8,64,64]{3,2,1,0:T(8,128)S(1)}, f32[2,8,64,64]{3,2,1,0:T(8,128)S(1)}, f32[2,8,4096]{2,1,0:T(8,128)}, f32[2,8,64,64]{3,2,1,0:T...) while((s32[]{:T(128)}, f32[2,8,64,64]{3,2,1,0:T(8,128)S(1)}, ...), condition=%wide.region_7.8_spmd.clone.clone, body=%wide.region_5.7_spmd.clone.clone.sunk | while | flops 1210646528 | bytes 27525276 | solution.py:100
  356.5 1.0 constant_dynamic-slice_fusion.5
  358.2 0.7 convolution_bitcast_fusion.40
  358.9 0.7 convolution_bitcast_fusion.41
  360.6 10.1 %all_to_all.161 = f32[2,8,64,128]{3,1,0,2:T(8,128)S(1)} all-to-all(f32[2,8,64,128]{3,1,0,2:T(8,128)S(1)} %copy.77), channel_id=1, replica_groups=mesh['band'=32,'fft'=8] {'fft'}, dimensions={2} | all-to-all | bytes 1048576 | tf_op jit(solution)/shard_map/while/body/eval_jaxpr/all_to_all | solution.py:70
  372.5 0.8 convolution_bitcast_fusion.45
  373.3 0.8 convolution_bitcast_fusion.44
  374.7 1.1 copy.78
  375.8 3.5 all-to-all-start.3
  379.3 7.0 all-to-all-done.3
  386.3 0.7 convolution_bitcast_fusion.46
  389.2 0.9 constant_dynamic-slice_fusion.5
  390.8 0.7 convolution_bitcast_fusion.40
  391.6 0.7 convolution_bitcast_fusion.41
  393.2 10.1 %all_to_all.161 = f32[2,8,64,128]{3,1,0,2:T(8,128)S(1)} all-to-all(f32[2,8,64,128]{3,1,0,2:T(8,128)S(1)} %copy.77), channel_id=1, replica_groups=mesh['band'=32,'fft'=8] {'fft'}, dimensions={2} | all-to-all | bytes 1048576 | tf_op jit(solution)/shard_map/while/body/eval_jaxpr/all_to_all | solution.py:70
  405.1 0.8 convolution_bitcast_fusion.45
  405.9 0.8 convolution_bitcast_fusion.44
  407.3 1.1 copy.78
  408.4 3.5 all-to-all-start.3
  411.9 7.0 all-to-all-done.3
  419.0 0.7 convolution_bitcast_fusion.46
  421.9 1.2 reshape.151
  423.0 0.9 reshape.150
  423.9 278.5 %all-reduce.6.cloned.1.call-done = f32[4,8,4096]{2,1,0:T(8,128)} async-done(((f32[4,8,4096]{2,1,0:T(8,128)}), f32[4,8,4096]{2,1,0:T(8,128)}) %all-reduce.6.cloned.1.call-update) | async-done | bytes 524304 | tf_op jit(solution)/shard_map/psum | solution.py:121
  702.4 1.9 copy.102
  (100 shorter events, 29.2 us)
Async XLA Ops:
  7.2 277.9 %all-reduce.8.cloned.1.call-start = ((), (), s32[]{:S(2)}) async-start(), calls=%async_computation.5 | async-start | bytes 2097152 | tf_op jit(solution)/shard_map/psum | solution.py:18
  10.3 692.1 %all-reduce.6.cloned.1.call-start = ((), (), s32[]{:S(2)}) async-start(), calls=%async_computation.4 | async-start | bytes 1048576 | tf_op jit(solution)/shard_map/psum | solution.py:121
  285.1 1.0 copy-start.1
  286.1 70.4 %copy-start = (f32[2,8,64,64]{3,2,1,0:T(8,128)S(1)}, f32[2,8,64,64]{3,2,1,0:T(8,128)}, u32[]{:S(2)}) copy-start(f32[2,8,64,64]{3,2,1,0:T(8,128)} %get-tuple-element.738) | copy-start | bytes 786436
  307.8 10.6 %all-to-all-start.1 = ((f32[2,64,8,128]{3,2,0,1:T(8,128)}), f32[2,64,8,128]{3,2,0,1:T(8,128)S(1)}, u32[]{:S(2)}, u32[]{:S(2)}) async-start(f32[2,64,8,128]{3,2,0,1:T(8,128)} %copy.72), calls=%async_computation.1 | async-start | bytes 1048576 | tf_op jit(solution)/shard_map/while/body/eval_jaxpr/all_to_all | solution.py:73
  320.2 1.0 copy-start.2
  321.5 0.8 copy-start.3
  342.0 10.6 %all-to-all-start.1 = ((f32[2,64,8,128]{3,2,0,1:T(8,128)}), f32[2,64,8,128]{3,2,0,1:T(8,128)S(1)}, u32[]{:S(2)}, u32[]{:S(2)}) async-start(f32[2,64,8,128]{3,2,0,1:T(8,128)} %copy.72), calls=%async_computation.1 | async-start | bytes 1048576 | tf_op jit(solution)/shard_map/while/body/eval_jaxpr/all_to_all | solution.py:73
  354.4 1.0 copy-start.2
  355.7 0.8 copy-start.3
  356.5 65.3 %copy-start.4 = (f32[2,8,64,64]{3,2,1,0:T(8,128)S(1)}, f32[2,8,64,64]{3,2,1,0:T(8,128)}, u32[]{:S(2)}) copy-start(f32[2,8,64,64]{3,2,1,0:T(8,128)} %get-tuple-element.380) | copy-start | bytes 786436
  375.8 10.6 %all-to-all-start.3 = ((f32[2,64,8,128]{3,2,0,1:T(8,128)}), f32[2,64,8,128]{3,2,0,1:T(8,128)S(1)}, u32[]{:S(2)}, u32[]{:S(2)}) async-start(f32[2,64,8,128]{3,2,0,1:T(8,128)} %copy.78), calls=%async_computation.3 | async-start | bytes 1048576 | tf_op jit(solution)/shard_map/while/body/eval_jaxpr/all_to_all | solution.py:73
  408.4 10.6 %all-to-all-start.3 = ((f32[2,64,8,128]{3,2,0,1:T(8,128)}), f32[2,64,8,128]{3,2,0,1:T(8,128)S(1)}, u32[]{:S(2)}, u32[]{:S(2)}) async-start(f32[2,64,8,128]{3,2,0,1:T(8,128)} %copy.78), calls=%async_computation.3 | async-start | bytes 1048576 | tf_op jit(solution)/shard_map/while/body/eval_jaxpr/all_to_all | solution.py:73
Sparse Core Ops, SparseCore 0:
  10.7 274.3 all-reduce.7
  423.2 279.1 all-reduce.5
where the time goes:
time: 712 us; the launch traced here: 711 us
  waiting for transfers between devices  581 us (82%)
  blocking collectives  43.3 us (6%)
  matrix products  28.9 us (4%)
  local copies, waits for them, and re-layouts  19.1 us (3%)
  between operations  14.1 us (2%)
  starting transfers between devices  14 us (2%)
  other arithmetic  10.4 us (1%)
    psum x1, waiting for transfers between devices, body(): window_total = lax.psum(window_part, 'band')  278 us
    psum x1, waiting for transfers between devices, broadcast(): return lax.psum(jnp.where(mine, value, jnp.zeros_like(value)), axis)  274 us
    all_to_all x4, blocking collectives, planes_potential(): lax.all_to_all(spectrum, 'fft', split_axis=2, concat_axis=1, tiled=True)  43.3 us
    all_to_all x4, waiting for transfers between devices, planes_potential(): lax.all_to_all(pencils, 'fft', split_axis=1, concat_axis=2, tiled=True)  28.1 us
  transfers between devices with their start and end apart: 6, of which 6 were waited for; matrix products, arithmetic and copies ran while one was open for 0% of the time, Pallas kernels for 0%

commit v1 on v0

v1 whole, which is shorter than its diff:
```python
import functools
import math

import jax
import jax.numpy as jnp
import ml_dtypes
import numpy as np
from jax import lax
from jax.experimental import pallas as pl
from jax.experimental.pallas import tpu as pltpu
from jax.sharding import PartitionSpec as P

GRID = 64
LANES = 128
PLANES = 8
HALF = 32
SPACING = 0.367
MIXING = 0.25
MESH = pl.DeviceIdType.MESH
BF16 = jnp.bfloat16
F32 = jnp.float32
UNROLL = 2


def split_table(table):
    high = table.astype(ml_dtypes.bfloat16)
    low = (table - high.astype(np.float64)).astype(ml_dtypes.bfloat16)
    return high, low


def make_tables():
    counter = np.arange(GRID)
    angles = (counter[:, None] * counter[None, :] % GRID) * (2.0 * np.pi / GRID)
    cosine, sine = np.cos(angles), np.sin(angles)
    depth = []
    for sign in (1.0, -1.0):
        table = np.block([[cosine, -sign * sine], [sign * sine, cosine]])
        high, low = split_table(table)
        row = np.concatenate([high, low], 1)
        depth.append(np.concatenate([row, row], 0))
    order = np.concatenate([np.arange(0, GRID, 2), np.arange(1, GRID, 2)])

    def stacked(rows, columns):
        table = np.concatenate(
            [cosine[np.ix_(rows, columns)], sine[np.ix_(rows, columns)]], 0
        )
        high, low = split_table(table)
        return np.concatenate([high, low, high, low], 1)

    return depth + [
        stacked(counter, order),
        stacked(counter, counter),
        stacked(order, counter),
    ]


def split_values(values):
    high = values.astype(BF16)
    low = (values - high.astype(F32)).astype(BF16)
    return high, low


def along_lanes(values, table):
    high, low = split_values(values)
    both = jnp.dot(jnp.concatenate([high, low], 1), table, preferred_element_type=F32)
    return both[:, :LANES] + both[:, LANES:]


def along_rows(first, second, table, sign):
    high, low = split_values(jnp.concatenate([first, second], 1))
    stack = jnp.concatenate([high, high, low, low], 0)
    both = jnp.dot(table, stack, preferred_element_type=F32)
    outs = []
    for index in range(2):
        columns = slice(index * LANES, (index + 1) * LANES)
        cos_part, sin_part = both[:GRID, columns], both[GRID:, columns]
        outs.append(cos_part + sign * pltpu.roll(sin_part, GRID, 1))
    return outs


def wait_for(ref, sem):
    pltpu.make_async_copy(ref, ref, sem).wait()


def kernel(
    nf, nq,
    orb_ref, fz_ref, iz_ref, fy_ref, fx_ref, iy_ref,
    local_ref, window_ref,
    obuf, dbuf, ktab, wbuf, fsend, frecv, bsend, brecv, part, pbuf, hbuf, rsbuf, acc, fin,
    sc_s, sc_r, ag_s, ag_r, cx_s, cx_r, f_s, f_r, b_s, b_r,
    p_s, p_r, rs_s, rs_r, ga_s, ga_r, fx_s, fx_r,
):
    band = lax.axis_index("band")
    me = lax.axis_index("fft")
    core = lax.rem(band, 2)
    chip = band // 2
    other = band + 1 - 2 * core
    second_root = nq
    root_chip = second_root // 2
    rows = 256 // nq

    barrier = pltpu.get_barrier_semaphore()

    def signal(b, f):
        pl.semaphore_signal(barrier, inc=1, device_id=(b, f), device_id_type=MESH)

    def greet_fft(step, carry):
        signal(band, lax.rem(me + step, nf))
        return carry

    def greet_band(step, carry):
        signal(2 * lax.rem(chip + step, nq) + core, me)
        return carry

    lax.fori_loop(1, nf, greet_fft, 0)
    lax.fori_loop(1, nq, greet_band, 0)
    signal(other, me)

    @pl.when(jnp.logical_and(core == 1, chip != root_chip))
    def _():
        signal(second_root, me)

    @pl.when(band == second_root)
    def _():
        def greet_odd(step, carry):
            signal(2 * lax.rem(chip + step, nq) + 1, me)
            return carry

        lax.fori_loop(1, nq, greet_odd, 0)

    extra = jnp.where(
        band == second_root, nq - 1, jnp.where(jnp.logical_and(core == 1, chip != root_chip), 1, 0)
    )
    pl.semaphore_wait(barrier, nf - 1 + nq - 1 + 1 + extra)

    @pl.when(band == 0)
    def _():
        pltpu.make_async_copy(
            orb_ref.at[:, pl.ds(0, rows), :], wbuf.at[pl.ds(0, 2), pl.ds(0, rows), :], sc_r
        ).start()

        def scatter(p, carry):
            piece = pl.ds(pl.multiple_of(p * rows, rows), rows)
            pltpu.make_async_remote_copy(
                orb_ref.at[:, piece, :], wbuf.at[pl.ds(0, 2), piece, :], sc_s, sc_r,
                device_id=(2 * p, me), device_id_type=MESH,
            ).start()
            return carry

        lax.fori_loop(1, nq, scatter, 0)

    @pl.when(band == second_root)
    def _():
        def scatter(p, carry):
            piece = pl.ds(pl.multiple_of(p * rows, rows), rows)
            pltpu.make_async_remote_copy(
                orb_ref.at[:, piece, :], wbuf.at[pl.ds(2, 2), piece, :], sc_s, sc_r,
                device_id=(2 * p + 1, me), device_id_type=MESH,
            ).start()
            return carry

        lax.fori_loop(0, nq, scatter, 0)

    lane = lax.broadcasted_iota(jnp.int32, (GRID, LANES), 1)
    low_lane = lane < GRID
    sign = jnp.where(low_lane, 1.0, -1.0).astype(F32)

    def fold(values):
        return jnp.where(2 * values < GRID, values, values - GRID)

    kz = fold(jnp.where(low_lane, lane, lane - GRID))
    kx = fold(lax.broadcasted_iota(jnp.int32, (GRID, LANES), 0))
    base = kx * kx + kz * kz
    factor = (2.0 * math.pi / (GRID * SPACING)) ** 2
    scale = -MIXING / GRID**3

    for row in range(GRID // nf):
        ky = fold(me * (GRID // nf) + row)
        squared = base + ky * ky
        clamped = jnp.maximum(squared, 1).astype(F32)
        ktab[row] = jnp.where(
            squared > 0, (4.0 * math.pi / factor * scale) / clamped, 0.0
        )

    half_lane = low_lane[:HALF]

    def pack_orbitals(x, carry):
        source = pl.ds(pl.multiple_of(x * HALF, HALF), HALF)
        first, second = orb_ref[0, source, :], orb_ref[1, source, :]
        start = pl.multiple_of(x * GRID, GRID)
        obuf[pl.ds(start, HALF), :] = jnp.where(half_lane, first, pltpu.roll(second, GRID, 1))
        obuf[pl.ds(start + HALF, HALF), :] = jnp.where(
            half_lane, pltpu.roll(first, GRID, 1), second
        )
        return carry

    lax.fori_loop(0, PLANES, pack_orbitals, 0)

    mine = pl.ds(2 * core, 2)
    wait_for(wbuf.at[pl.ds(0, 2), pl.ds(0, rows), :], sc_r)
    own_piece = pl.ds(pl.multiple_of(chip * rows, rows), rows)

    def gather(step, carry):
        p = lax.rem(chip + step, nq)
        pltpu.make_async_remote_copy(
            wbuf.at[mine, own_piece, :], wbuf.at[mine, own_piece, :], ag_s, ag_r,
            device_id=(2 * p + core, me), device_id_type=MESH,
        ).start()
        return carry

    lax.fori_loop(1, nq, gather, 0)
    wait_for(wbuf.at[pl.ds(0, 2), pl.ds(0, (nq - 1) * rows), :], ag_r)
    cross = pltpu.make_async_remote_copy(
        wbuf.at[mine], wbuf.at[mine], cx_s, cx_r, device_id=(other, me), device_id_type=MESH
    )
    cross.start()

    block = GRID * PLANES // nf

    def exchange(source, target, send_sem, recv_sem, k):
        own = pl.ds(pl.multiple_of(me * block, block), block)
        pltpu.make_async_copy(source.at[k, own, :], target.at[k, me], recv_sem.at[k]).start()

        def send(step, carry):
            p = lax.rem(me + step, nf)
            pltpu.make_async_remote_copy(
                source.at[k, pl.ds(pl.multiple_of(p * block, block), block), :],
                target.at[k, me], send_sem.at[k], recv_sem.at[k],
                device_id=(band, p), device_id_type=MESH,
            ).start()
            return carry

        lax.fori_loop(1, nf, send, 0)

    def forward(k):
        j = lax.rem(2 * core + k, 4)

        def step(i, carry):
            for inner in range(2):
                x = 2 * i + inner
                values = wbuf[j, pl.ds(pl.multiple_of(x * HALF, HALF), HALF), :]
                turned = pltpu.roll(values, GRID, 1)
                start = pl.multiple_of(x * GRID, GRID)
                dbuf[k, pl.ds(start, HALF), :] = jnp.where(half_lane, values, turned)
                dbuf[k, pl.ds(start + HALF, HALF), :] = jnp.where(half_lane, turned, values)
            both = pl.ds(pl.multiple_of(i * 2 * GRID, 2 * GRID), 2 * GRID)
            field = along_lanes(obuf[both, :] * dbuf[k, both, :], fz_ref[...])
            outs = along_rows(field[:GRID], field[GRID:], fy_ref[...], sign)
            for inner in range(2):
                fsend[k, pl.ds(2 * i + inner, GRID, stride=PLANES), :] = outs[inner]
            return carry

        lax.fori_loop(0, PLANES // 2, step, 0, unroll=UNROLL)
        exchange(fsend, frecv, f_s, f_r, k)

    def middle(k):
        wait_for(frecv.at[k], f_r.at[k])

        def step(i, carry):
            pair = []
            for inner in range(2):
                start = pl.multiple_of((2 * i + inner) * PLANES, PLANES)
                pair.append(frecv[k, :, pl.ds(start, PLANES), :].reshape(GRID, LANES))
            outs = along_rows(pair[0], pair[1], fx_ref[...], sign)
            outs = [outs[inner] * ktab[2 * i + inner] for inner in range(2)]
            outs = along_rows(outs[0], outs[1], fx_ref[...], -sign)
            for inner in range(2):
                bsend[k, pl.ds(2 * i + inner, GRID, stride=PLANES), :] = outs[inner]
            return carry

        lax.fori_loop(0, GRID // nf // 2, step, 0, unroll=UNROLL)
        exchange(bsend, brecv, b_s, b_r, k)

    def backward(k):
        wait_for(brecv.at[k], b_r.at[k])

        def step(i, carry):
            pair = []
            for inner in range(2):
                start = pl.multiple_of((2 * i + inner) * PLANES, PLANES)
                pair.append(brecv[k, :, pl.ds(start, PLANES), :].reshape(GRID, LANES))
            outs = along_rows(pair[0], pair[1], iy_ref[...], -sign)
            potential = along_lanes(jnp.concatenate(outs, 0), iz_ref[...])
            both = pl.ds(pl.multiple_of(i * 2 * GRID, 2 * GRID), 2 * GRID)
            term = dbuf[k, both, :] * potential
            if k == 0:
                acc[both, :] = term
            else:
                acc[both, :] += term
            product = obuf[both, :] * potential
            total = product + pltpu.roll(product, GRID, 1)
            for inner in range(2):
                start = inner * GRID
                part[k, pl.ds(pl.multiple_of((2 * i + inner) * HALF, HALF), HALF), :] = jnp.where(
                    half_lane, total[start:start + HALF], total[start + HALF:start + GRID]
                )
            return carry

        lax.fori_loop(0, PLANES // 2, step, 0, unroll=UNROLL)

    def to_partner(source, target, send_sem, recv_sem):
        pltpu.make_async_remote_copy(
            source, target, send_sem, recv_sem, device_id=(other, me), device_id_type=MESH
        ).start()

    def scatter_sum(k):
        wait_for(pbuf.at[k], p_r.at[k])
        hbuf[k] = part[k + 2] + pbuf[k]
        rsbuf[k, chip] = hbuf[k, own_piece, :]

        def send(step, carry):
            p = lax.rem(chip + step, nq)
            pltpu.make_async_remote_copy(
                hbuf.at[k, pl.ds(pl.multiple_of(p * rows, rows), rows), :], rsbuf.at[k, chip],
                rs_s.at[k], rs_r.at[k], device_id=(2 * p + core, me), device_id_type=MESH,
            ).start()
            return carry

        lax.fori_loop(1, nq, send, 0)

    theirs = 2 - 2 * core

    def gather_sum(k):
        wait_for(rsbuf.at[k, pl.ds(0, nq - 1)], rs_r.at[k])
        total = rsbuf[k, 0]
        for slot in range(1, nq):
            total = total + rsbuf[k, slot]
        fin[theirs + k, own_piece, :] = total

        def send(step, carry):
            p = lax.rem(chip + step, nq)
            pltpu.make_async_remote_copy(
                fin.at[theirs + k, own_piece, :], fin.at[theirs + k, own_piece, :],
                ga_s.at[k], ga_r.at[k], device_id=(2 * p + core, me), device_id_type=MESH,
            ).start()
            return carry

        lax.fori_loop(1, nq, send, 0)

    def share_sum(k):
        wait_for(fin.at[k, pl.ds(0, (nq - 1) * rows), :], ga_r.at[k])
        to_partner(fin.at[theirs + k], fin.at[theirs + k], fx_s.at[k], fx_r.at[k])

    forward(0)
    forward(1)
    wait_for(wbuf.at[pl.ds(0, 2)], cx_r)
    forward(2)
    forward(3)
    for k in range(4):
        middle(k)
    for k in range(2):
        backward(k)
        to_partner(part.at[k], pbuf.at[k], p_s.at[k], p_r.at[k])
    for k in range(2):
        backward(k + 2)
        scatter_sum(k)

    def unpack(x, carry):
        start = pl.multiple_of(x * GRID, GRID)
        even, odd = acc[pl.ds(start, HALF), :], acc[pl.ds(start + HALF, HALF), :]
        target = pl.ds(pl.multiple_of(x * HALF, HALF), HALF)
        local_ref[0, target, :] = jnp.where(half_lane, even, pltpu.roll(odd, GRID, 1))
        local_ref[1, target, :] = jnp.where(half_lane, pltpu.roll(even, GRID, 1), odd)
        return carry

    lax.fori_loop(0, PLANES, unpack, 0)
    for k in range(2):
        gather_sum(k)
    for k in range(2):
        share_sum(k)

    @pl.when(band == 0)
    def _():
        wait_for(wbuf.at[pl.ds(0, 2), pl.ds(0, (nq - 1) * rows), :], sc_s)

    @pl.when(band == second_root)
    def _():
        wait_for(wbuf.at[pl.ds(0, 2)], sc_s)

    wait_for(wbuf.at[pl.ds(0, 2), pl.ds(0, (nq - 1) * rows), :], ag_s)
    wait_for(wbuf.at[pl.ds(0, 2)], cx_s)
    for k in range(4):
        wait_for(frecv.at[k, pl.ds(0, nf - 1)], f_s.at[k])
        wait_for(brecv.at[k, pl.ds(0, nf - 1)], b_s.at[k])
    for k in range(2):
        wait_for(pbuf.at[k], p_s.at[k])
        wait_for(rsbuf.at[k, pl.ds(0, nq - 1)], rs_s.at[k])
        wait_for(fin.at[k, pl.ds(0, (nq - 1) * rows), :], ga_s.at[k])
        wait_for(fin.at[k], fx_s.at[k])
        wait_for(fin.at[k], fx_r.at[k])
    window_ref[...] = fin[...]


def body(orbitals):
    nf = lax.axis_size("fft")
    nq = lax.axis_size("band") // 2
    rows = 256 // nq
    block = GRID * PLANES // nf
    tables = [jnp.asarray(table) for table in make_tables()]
    dma, vmem = pltpu.SemaphoreType.DMA, pltpu.VMEM
    local_out, window_out = pl.pallas_call(
        functools.partial(kernel, nf, nq),
        out_shape=(
            jax.ShapeDtypeStruct((2, PLANES * HALF, LANES), F32),
            jax.ShapeDtypeStruct((4, PLANES * HALF, LANES), F32),
        ),
        in_specs=[pl.BlockSpec(memory_space=vmem)] * 6,
        out_specs=(pl.BlockSpec(memory_space=vmem),) * 2,
        scratch_shapes=[
            vmem((PLANES * GRID, LANES), F32),
            vmem((4, PLANES * GRID, LANES), F32),
            vmem((GRID // nf, GRID, LANES), F32),
            vmem((4, 256, LANES), F32),
            vmem((4, PLANES * GRID, LANES), F32),
            vmem((4, nf, block, LANES), F32),
            vmem((4, PLANES * GRID, LANES), F32),
            vmem((4, nf, block, LANES), F32),
            vmem((4, 256, LANES), F32),
            vmem((2, 256, LANES), F32),
            vmem((2, 256, LANES), F32),
            vmem((2, nq, rows, LANES), F32),
            vmem((PLANES * GRID, LANES), F32),
            vmem((4, 256, LANES), F32),
            dma, dma, dma, dma, dma, dma,
            dma((4,)), dma((4,)), dma((4,)), dma((4,)),
            dma((2,)), dma((2,)), dma((2,)), dma((2,)),
            dma((2,)), dma((2,)), dma((2,)), dma((2,)),
        ],
        compiler_params=pltpu.CompilerParams(
            collective_id=0, has_side_effects=True, vmem_limit_bytes=40 * 1024 * 1024
        ),
        cost_estimate=pl.CostEstimate(
            flops=6 * 4 * 2 * 512 * 256 * 256, bytes_accessed=1 << 20, transcendentals=0
        ),
    )(orbitals.reshape(2, PLANES * HALF, LANES), *tables)
    return (
        local_out.reshape(2, PLANES, GRID * GRID),
        window_out.reshape(4, PLANES, GRID * GRID),
    )


def solution(mesh):
    return jax.shard_map(
        body,
        mesh=mesh,
        in_specs=(P("band", "fft", None),),
        out_specs=(P("band", "fft", None), P(None, "fft", None)),
        check_vma=False,
    )
```

time: 712 us -> 74.5 us (0.10)
  waiting for transfers between devices: 581 us -> 0 us
  Pallas kernels: 0 us -> 70.9 us
  blocking collectives: 43.3 us -> 0 us
  matrix products: 28.9 us -> 0 us
  local copies, waits for them, and re-layouts: 19.1 us -> 2.76 us
  starting transfers between devices: 14 us -> 0 us
  between operations: 14.1 us -> 0.72 us
  other arithmetic: 10.4 us -> 0 us
    psum x2 -> x0, waiting for transfers between devices: 552 us -> none  [the longest x1 278 us: body(): window_total = lax.psum(window_part, 'band')]
    pallas_call x0 -> x1, Pallas kernels: none -> 70.9 us  [body(): pl.pallas_call(functools.partial(kernel, nf, nq), out_shape=(jax.ShapeDty...]
    all_to_all x4 -> x0, blocking collectives: 43.3 us -> none  [planes_potential(): lax.all_to_all(spectrum, 'fft', split_axis=2, concat_axis=1, tiled=True)]
    dot_general x40 -> x0, matrix products: 28.9 us -> none  [the longest x16 12.1 us: along_axis(): sin_part = jnp.einsum(pattern, sine_table, packed_field, precision=highest)]
    all_to_all x4 -> x0, waiting for transfers between devices: 28.1 us -> none  [planes_potential(): lax.all_to_all(pencils, 'fft', split_axis=1, concat_axis=2, tiled=True)]
    all_to_all x4 -> x0, starting transfers between devices: 14 us -> none  [planes_potential(): lax.all_to_all(pencils, 'fft', split_axis=1, concat_axis=2, tiled=True)]
  transfers between devices with their start and end apart: 6 -> 0, of which waited for: 6 -> 0; matrix products, arithmetic and copies ran while one was open for 0% -> 0% of each run, Pallas kernels for 0% -> 0%
where the time goes in v1:
time: 74.5 us; the launch traced here: 74.4 us
  Pallas kernels  70.9 us (95%)
  local copies, waits for them, and re-layouts  2.76 us (4%)
    pallas_call x1, Pallas kernels, body(): pl.pallas_call(functools.partial(kernel, nf, nq), out_shape=(jax.ShapeDty...  70.9 us

profile of v1, /device:TPU:1, one launch (start us, length us, event | category | flops | bytes accessed | tf_op | source)
XLA Modules:
  0.0 74.4 jit_solution(8873445625846153952)
XLA Ops:
  0.6 0.0 copy-start
  0.6 0.0 copy-start.1
  0.7 0.0 copy-start.2
  0.7 0.0 copy-start.3
  0.7 0.0 copy-start.4
  0.7 1.1 %reshape.13.orb_ref = f32[2,256,128]{2,1,0:T(8,128)S(1)} reshape(f32[2,8,4096]{2,1,0:T(8,128)} %param.6) | data formatting | bytes 524288 | tf_op jit(solution)/shard_map/reshape | solution.py:435
  1.8 0.0 copy-done
  1.8 0.0 copy-done.1
  1.8 0.0 copy-done.2
  1.8 0.0 copy-done.3
  1.8 0.0 copy-done.4
  1.8 70.9 %shard_map.77 = (f32[2,256,128]{2,1,0:T(8,128)S(1)}, f32[4,256,128]{2,1,0:T(8,128)S(1)}) custom-call(f32[2,256,128]{2,1,0:T(8,128)S(1)} %reshape.13.orb_ref, bf16[256,256]{1,0:T(8,128)(2,1)S(1)} %copy-done.1, bf16[256,256]{1,0:T(8,128)(2,1)S(1)} %copy-done, bf16[128,256]{1,0:T(8,128)(2,1)S(1)} %copy-done.4, bf16[128,256]{1,0:T(8,128)(2,1)S(1)} %copy-done.3, ...), custom_call_target="tpu_custom_call" | custom-call | flops 1610612736 | bytes 1048576 | tf_op jit(solution)/shard_map/pallas_call | solution.py:401
  72.7 0.8 %reshape.14 = f32[2,8,4096]{2,1,0:T(8,128)} reshape(f32[2,256,128]{2,1,0:T(8,128)S(1)} %get-tuple-element.4) | data formatting | bytes 524288 | tf_op jit(solution)/shard_map/reshape | solution.py:437
  73.5 0.9 %reshape.15 = f32[4,8,4096]{2,1,0:T(8,128)} reshape(f32[4,256,128]{2,1,0:T(8,128)S(1)} %get-tuple-element.5) | data formatting | bytes 1048576 | tf_op jit(solution)/shard_map/reshape | solution.py:438
Async XLA Ops:
  0.6 1.1 %copy-start = (bf16[256,256]{1,0:T(8,128)(2,1)S(1)}, bf16[256,256]{1,0:T(8,128)(2,1)}, u32[]{:S(2)}) copy-start(bf16[256,256]{1,0:T(8,128)(2,1)} %constant.11.clone.iz_ref) | copy-start | bytes 393220
  0.6 1.1 %copy-start.1 = (bf16[256,256]{1,0:T(8,128)(2,1)S(1)}, bf16[256,256]{1,0:T(8,128)(2,1)}, u32[]{:S(2)}) copy-start(bf16[256,256]{1,0:T(8,128)(2,1)} %constant.10.clone.fz_ref) | copy-start | bytes 393220
  0.7 1.1 %copy-start.2 = (bf16[128,256]{1,0:T(8,128)(2,1)S(1)}, bf16[128,256]{1,0:T(8,128)(2,1)}, u32[]{:S(2)}) copy-start(bf16[128,256]{1,0:T(8,128)(2,1)} %constant.14.clone.iy_ref) | copy-start | bytes 196612
  0.7 1.1 %copy-start.3 = (bf16[128,256]{1,0:T(8,128)(2,1)S(1)}, bf16[128,256]{1,0:T(8,128)(2,1)}, u32[]{:S(2)}) copy-start(bf16[128,256]{1,0:T(8,128)(2,1)} %constant.13.clone.fx_ref) | copy-start | bytes 196612
  0.7 1.1 %copy-start.4 = (bf16[128,256]{1,0:T(8,128)(2,1)S(1)}, bf16[128,256]{1,0:T(8,128)(2,1)}, u32[]{:S(2)}) copy-start(bf16[128,256]{1,0:T(8,128)(2,1)} %constant.12.clone.fy_ref) | copy-start | bytes 196612

commit v2 on v1

v2 whole, which is shorter than its diff:
```python
import functools
import math

import jax
import jax.numpy as jnp
import ml_dtypes
import numpy as np
from jax import lax
from jax.experimental import pallas as pl
from jax.experimental.pallas import tpu as pltpu
from jax.sharding import PartitionSpec as P

GRID = 64
LANES = 128
PLANES = 8
HALF = 32
SPACING = 0.367
MIXING = 0.25
MESH = pl.DeviceIdType.MESH
BF16 = jnp.bfloat16
F32 = jnp.float32


def split_table(table):
    high = table.astype(ml_dtypes.bfloat16)
    low = (table - high.astype(np.float64)).astype(ml_dtypes.bfloat16)
    return high, low


def make_tables():
    counter = np.arange(GRID)
    angles = (counter[:, None] * counter[None, :] % GRID) * (2.0 * np.pi / GRID)
    cosine, sine = np.cos(angles), np.sin(angles)
    depth = []
    for sign in (1.0, -1.0):
        table = np.block([[cosine, -sign * sine], [sign * sine, cosine]])
        high, low = split_table(table)
        row = np.concatenate([high, low], 1)
        depth.append(np.concatenate([row, row], 0))
    order = np.concatenate([np.arange(0, GRID, 2), np.arange(1, GRID, 2)])

    def stacked(rows, columns):
        table = np.concatenate(
            [cosine[np.ix_(rows, columns)], sine[np.ix_(rows, columns)]], 0
        )
        high, low = split_table(table)
        return np.concatenate([high, low, high, low], 1)

    return depth + [
        stacked(counter, order),
        stacked(counter, counter),
        stacked(order, counter),
    ]


def split_values(values):
    high = values.astype(BF16)
    low = (values - high.astype(F32)).astype(BF16)
    return high, low


def along_lanes(values, table):
    high, low = split_values(values)
    both = jnp.dot(jnp.concatenate([high, low], 1), table, preferred_element_type=F32)
    return both[:, :LANES] + both[:, LANES:]


def along_rows(first, second, table, sign):
    high, low = split_values(jnp.concatenate([first, second], 1))
    stack = jnp.concatenate([high, high, low, low], 0)
    both = jnp.dot(table, stack, preferred_element_type=F32)
    outs = []
    for index in range(2):
        columns = slice(index * LANES, (index + 1) * LANES)
        cos_part, sin_part = both[:GRID, columns], both[GRID:, columns]
        outs.append(cos_part + sign * pltpu.roll(sin_part, GRID, 1))
    return outs


def loop(first, last, step):
    def advance(index, carry):
        step(index)
        return carry

    lax.fori_loop(first, last, advance, 0, unroll=last - first)


def wait_for(ref, sem):
    pltpu.make_async_copy(ref, ref, sem).wait()


def kernel(
    nf, nq,
    orb_hbm, fz_hbm, iz_hbm, fy_hbm, fx_hbm, iy_hbm,
    local_ref, window_ref,
    orb, fz, iz, fy, fx, iy,
    obuf, dbuf, ktab, wbuf, fsend, frecv, bsend, brecv, part, pbuf, hbuf, rsbuf, acc, fin,
    in_sem, table_sem, sc_s, sc_r, ag_s, ag_r, cx_s, cx_r, f_s, f_r, b_s, b_r,
    p_s, p_r, rs_s, rs_r, ga_s, ga_r, fx_s, fx_r,
):
    band = lax.axis_index("band")
    me = lax.axis_index("fft")
    core = lax.rem(band, 2)
    chip = band // 2
    other = band + 1 - 2 * core
    second_root = nq
    root_chip = second_root // 2
    rows = 256 // nq
    columns = 2
    levels = nq // columns
    level, column = chip // columns, lax.rem(chip, columns)
    width = GRID * GRID // levels

    barrier = pltpu.get_barrier_semaphore()

    def signal(b, f):
        pl.semaphore_signal(barrier, inc=1, device_id=(b, f), device_id_type=MESH)

    @pl.when(jnp.logical_and(core == 1, chip != root_chip))
    def _():
        signal(second_root, me)

    loop(1, nq, lambda step: signal(2 * lax.rem(chip + step, nq) + core, me))
    loop(1, nf, lambda step: signal(band, lax.rem(me + step, nf)))
    signal(other, me)

    @pl.when(band == second_root)
    def _():
        loop(1, nq, lambda step: signal(2 * lax.rem(chip + step, nq) + 1, me))

    loads = [pltpu.make_async_copy(orb_hbm, orb, in_sem)]
    loads += [
        pltpu.make_async_copy(source, target, table_sem.at[index])
        for index, (source, target) in enumerate(
            ((fz_hbm, fz), (iz_hbm, iz), (fy_hbm, fy), (fx_hbm, fx), (iy_hbm, iy))
        )
    ]
    for load in loads:
        load.start()
    loads[0].wait()

    extra = jnp.where(
        band == second_root, nq - 1, jnp.where(jnp.logical_and(core == 1, chip != root_chip), 1, 0)
    )
    pl.semaphore_wait(barrier, nf - 1 + nq - 1 + 1 + extra)

    def span(place):
        return pl.ds(pl.multiple_of(place * width, width), width)

    def scatter(window, root, p):
        piece = span(p // columns)
        pltpu.make_async_remote_copy(
            orb.at[window, :, piece], wbuf.at[2 * root + window, :, piece],
            sc_s.at[window], sc_r.at[window],
            device_id=(2 * p + root, me), device_id_type=MESH,
        ).start()

    @pl.when(band == 0)
    def _():
        for window in range(2):
            pltpu.make_async_copy(
                orb.at[window, :, pl.ds(0, width)], wbuf.at[window, :, pl.ds(0, width)],
                sc_r.at[window],
            ).start()
            loop(1, nq, lambda p: scatter(window, 0, p))

    @pl.when(band == second_root)
    def _():
        for window in range(2):
            loop(0, nq, lambda p: scatter(window, 1, p))

    lane = lax.broadcasted_iota(jnp.int32, (GRID, LANES), 1)
    low_lane = lane < GRID
    sign = jnp.where(low_lane, 1.0, -1.0).astype(F32)

    def fold(values):
        return jnp.where(2 * values < GRID, values, values - GRID)

    kz = fold(jnp.where(low_lane, lane, lane - GRID))
    kx = fold(lax.broadcasted_iota(jnp.int32, (GRID, LANES), 0))
    base = kx * kx + kz * kz
    factor = (2.0 * math.pi / (GRID * SPACING)) ** 2
    scale = -MIXING / GRID**3

    for row in range(GRID // nf):
        ky = fold(me * (GRID // nf) + row)
        squared = base + ky * ky
        clamped = jnp.maximum(squared, 1).astype(F32)
        ktab[row] = jnp.where(
            squared > 0, (4.0 * math.pi / factor * scale) / clamped, 0.0
        )

    tile_lane, half_lane = low_lane[:PLANES], low_lane[:HALF]

    def tile(t):
        return pl.ds(pl.multiple_of(t * LANES, LANES), LANES)

    def pack_orbitals(t):
        first, second = orb[0, :, tile(t)], orb[1, :, tile(t)]
        obuf[pl.ds(t, PLANES, stride=GRID), :] = jnp.where(
            tile_lane, first, pltpu.roll(second, GRID, 1)
        )
        obuf[pl.ds(t + HALF, PLANES, stride=GRID), :] = jnp.where(
            tile_lane, pltpu.roll(first, GRID, 1), second
        )

    loop(0, HALF, pack_orbitals)
    for load in loads[1:]:
        load.wait()

    def gather(window):
        mine = wbuf.at[2 * core + window, :, span(level)]
        wait_for(wbuf.at[window, :, pl.ds(0, width)], sc_r.at[window])

        def send(step):
            p = lax.rem(level + step, levels) * columns + column
            pltpu.make_async_remote_copy(
                mine, mine, ag_s.at[window], ag_r.at[window],
                device_id=(2 * p + core, me), device_id_type=MESH,
            ).start()

        loop(1, levels, send)

    def cross(window):
        wait_for(wbuf.at[window, :, pl.ds(0, (levels - 1) * width)], ag_r.at[window])
        whole = wbuf.at[2 * core + window]
        pltpu.make_async_remote_copy(
            whole, whole, cx_s.at[window], cx_r.at[window],
            device_id=(other, me), device_id_type=MESH,
        ).start()

    block = GRID * PLANES // nf

    def exchange(source, target, send_sem, recv_sem, k):
        own = pl.ds(pl.multiple_of(me * block, block), block)
        pltpu.make_async_copy(source.at[k, own, :], target.at[k, me], recv_sem.at[k]).start()

        def send(step):
            p = lax.rem(me + step, nf)
            pltpu.make_async_remote_copy(
                source.at[k, pl.ds(pl.multiple_of(p * block, block), block), :],
                target.at[k, me], send_sem.at[k], recv_sem.at[k],
                device_id=(band, p), device_id_type=MESH,
            ).start()

        loop(1, nf, send)

    def forward(k):
        j = lax.rem(2 * core + k, 4)

        def widen(t):
            values = wbuf[j, :, tile(t)]
            turned = pltpu.roll(values, GRID, 1)
            dbuf[k, pl.ds(t, PLANES, stride=GRID), :] = jnp.where(tile_lane, values, turned)
            dbuf[k, pl.ds(t + HALF, PLANES, stride=GRID), :] = jnp.where(
                tile_lane, turned, values
            )

        loop(0, HALF, widen)

        def step(i):
            both = pl.ds(pl.multiple_of(i * 2 * GRID, 2 * GRID), 2 * GRID)
            field = along_lanes(obuf[both, :] * dbuf[k, both, :], fz[...])
            outs = along_rows(field[:GRID], field[GRID:], fy[...], sign)
            for inner in range(2):
                fsend[k, pl.ds(2 * i + inner, GRID, stride=PLANES), :] = outs[inner]

        loop(0, PLANES // 2, step)
        exchange(fsend, frecv, f_s, f_r, k)

    def middle(k):
        wait_for(frecv.at[k], f_r.at[k])

        def step(i):
            pair = []
            for inner in range(2):
                start = pl.multiple_of((2 * i + inner) * PLANES, PLANES)
                pair.append(frecv[k, :, pl.ds(start, PLANES), :].reshape(GRID, LANES))
            outs = along_rows(pair[0], pair[1], fx[...], sign)
            outs = [outs[inner] * ktab[2 * i + inner] for inner in range(2)]
            outs = along_rows(outs[0], outs[1], fx[...], -sign)
            for inner in range(2):
                bsend[k, pl.ds(2 * i + inner, GRID, stride=PLANES), :] = outs[inner]

        loop(0, GRID // nf // 2, step)
        exchange(bsend, brecv, b_s, b_r, k)

    def backward(k):
        wait_for(brecv.at[k], b_r.at[k])

        def step(i):
            pair = []
            for inner in range(2):
                start = pl.multiple_of((2 * i + inner) * PLANES, PLANES)
                pair.append(brecv[k, :, pl.ds(start, PLANES), :].reshape(GRID, LANES))
            outs = along_rows(pair[0], pair[1], iy[...], -sign)
            potential = along_lanes(jnp.concatenate(outs, 0), iz[...])
            both = pl.ds(pl.multiple_of(i * 2 * GRID, 2 * GRID), 2 * GRID)
            term = dbuf[k, both, :] * potential
            if k == 0:
                acc[both, :] = term
            else:
                acc[both, :] += term
            product = obuf[both, :] * potential
            total = product + pltpu.roll(product, GRID, 1)
            for inner in range(2):
                start = inner * GRID
                part[k, pl.ds(2 * i + inner, HALF, stride=PLANES), :] = jnp.where(
                    half_lane, total[start:start + HALF], total[start + HALF:start + GRID]
                )

        loop(0, PLANES // 2, step)

    own_piece = pl.ds(pl.multiple_of(chip * rows, rows), rows)

    def to_partner(source, target, send_sem, recv_sem):
        pltpu.make_async_remote_copy(
            source, target, send_sem, recv_sem, device_id=(other, me), device_id_type=MESH
        ).start()

    def scatter_sum(k):
        wait_for(pbuf.at[k], p_r.at[k])
        hbuf[k] = part[k + 2] + pbuf[k]
        rsbuf[k, chip] = hbuf[k, own_piece, :]

        def send(step):
            p = lax.rem(chip + step, nq)
            pltpu.make_async_remote_copy(
                hbuf.at[k, pl.ds(pl.multiple_of(p * rows, rows), rows), :], rsbuf.at[k, chip],
                rs_s.at[k], rs_r.at[k], device_id=(2 * p + core, me), device_id_type=MESH,
            ).start()

        loop(1, nq, send)

    theirs = 2 - 2 * core

    def gather_sum(k):
        wait_for(rsbuf.at[k, pl.ds(0, nq - 1)], rs_r.at[k])
        total = rsbuf[k, 0]
        for slot in range(1, nq):
            total = total + rsbuf[k, slot]
        fin[theirs + k, own_piece, :] = total

        def send(step):
            p = lax.rem(chip + step, nq)
            pltpu.make_async_remote_copy(
                fin.at[theirs + k, own_piece, :], fin.at[theirs + k, own_piece, :],
                ga_s.at[k], ga_r.at[k], device_id=(2 * p + core, me), device_id_type=MESH,
            ).start()

        loop(1, nq, send)

    def share_sum(k):
        wait_for(fin.at[k, pl.ds(0, (nq - 1) * rows), :], ga_r.at[k])
        to_partner(fin.at[theirs + k], fin.at[theirs + k], fx_s.at[k], fx_r.at[k])

    def write_window(j, t):
        start = pl.multiple_of(t * PLANES, PLANES)
        window_ref[j, :, tile(t)] = fin[j, pl.ds(start, PLANES), :]

    gather(0)
    gather(1)
    for window in range(2):
        cross(window)
        forward(window)
    for window in range(2):
        wait_for(wbuf.at[window], cx_r.at[window])
        forward(window + 2)
    for k in range(4):
        middle(k)
    for k in range(2):
        backward(k)
        to_partner(part.at[k], pbuf.at[k], p_s.at[k], p_r.at[k])
    for k in range(2):
        backward(k + 2)
        scatter_sum(k)

    def unpack(t):
        even = acc[pl.ds(t, PLANES, stride=GRID), :]
        odd = acc[pl.ds(t + HALF, PLANES, stride=GRID), :]
        local_ref[0, :, tile(t)] = jnp.where(tile_lane, even, pltpu.roll(odd, GRID, 1))
        local_ref[1, :, tile(t)] = jnp.where(tile_lane, pltpu.roll(even, GRID, 1), odd)

    loop(0, HALF, unpack)
    for k in range(2):
        gather_sum(k)
    for k in range(2):
        share_sum(k)

    @pl.when(band == 0)
    def _():
        for window in range(2):
            sent = (nq - 1) * PLANES * width // LANES
            wait_for(fsend.at[0, pl.ds(0, sent), :], sc_s.at[window])

    @pl.when(band == second_root)
    def _():
        for window in range(2):
            sent = nq * PLANES * width // LANES
            wait_for(fsend.at[0, pl.ds(0, sent), :], sc_s.at[window])

    for window in range(2):
        wait_for(wbuf.at[window, :, pl.ds(0, (levels - 1) * width)], ag_s.at[window])
        wait_for(wbuf.at[window], cx_s.at[window])
    for k in range(4):
        wait_for(frecv.at[k, pl.ds(0, nf - 1)], f_s.at[k])
        wait_for(brecv.at[k, pl.ds(0, nf - 1)], b_s.at[k])
    for k in range(2):
        wait_for(pbuf.at[k], p_s.at[k])
        wait_for(rsbuf.at[k, pl.ds(0, nq - 1)], rs_s.at[k])
        wait_for(fin.at[k, pl.ds(0, (nq - 1) * rows), :], ga_s.at[k])
        wait_for(fin.at[k], fx_s.at[k])
        wait_for(fin.at[k], fx_r.at[k])
    for j in range(4):
        loop(0, HALF, functools.partial(write_window, j))


def body(orbitals):
    nf = lax.axis_size("fft")
    nq = lax.axis_size("band") // 2
    rows = 256 // nq
    block = GRID * PLANES // nf
    tables = [jnp.asarray(table) for table in make_tables()]
    dma, vmem = pltpu.SemaphoreType.DMA, pltpu.VMEM
    local_out, window_out = pl.pallas_call(
        functools.partial(kernel, nf, nq),
        out_shape=(
            jax.ShapeDtypeStruct((2, PLANES, GRID * GRID), F32),
            jax.ShapeDtypeStruct((4, PLANES, GRID * GRID), F32),
        ),
        in_specs=[pl.BlockSpec(memory_space=pltpu.HBM)] * 6,
        out_specs=(pl.BlockSpec(memory_space=vmem),) * 2,
        scratch_shapes=[
            vmem((2, PLANES, GRID * GRID), F32),
            vmem((256, 256), BF16),
            vmem((256, 256), BF16),
            vmem((128, 256), BF16),
            vmem((128, 256), BF16),
            vmem((128, 256), BF16),
            vmem((PLANES * GRID, LANES), F32),
            vmem((4, PLANES * GRID, LANES), F32),
            vmem((GRID // nf, GRID, LANES), F32),
            vmem((4, PLANES, GRID * GRID), F32),
            vmem((4, PLANES * GRID, LANES), F32),
            vmem((4, nf, block, LANES), F32),
            vmem((4, PLANES * GRID, LANES), F32),
            vmem((4, nf, block, LANES), F32),
            vmem((4, 256, LANES), F32),
            vmem((2, 256, LANES), F32),
            vmem((2, 256, LANES), F32),
            vmem((2, nq, rows, LANES), F32),
            vmem((PLANES * GRID, LANES), F32),
            vmem((4, 256, LANES), F32),
            dma, dma((5,)), dma((2,)), dma((2,)), dma((2,)), dma((2,)), dma((2,)), dma((2,)),
            dma((4,)), dma((4,)), dma((4,)), dma((4,)),
            dma((2,)), dma((2,)), dma((2,)), dma((2,)),
            dma((2,)), dma((2,)), dma((2,)), dma((2,)),
        ],
        compiler_params=pltpu.CompilerParams(
            collective_id=0, has_side_effects=True, vmem_limit_bytes=56 * 1024 * 1024
        ),
        cost_estimate=pl.CostEstimate(
            flops=6 * 4 * 2 * 512 * 256 * 256, bytes_accessed=1 << 20, transcendentals=0
        ),
    )(orbitals, *tables)
    return local_out, window_out


def solution(mesh):
    return jax.shard_map(
        body,
        mesh=mesh,
        in_specs=(P("band", "fft", None),),
        out_specs=(P("band", "fft", None), P(None, "fft", None)),
        check_vma=False,
    )
```

time: 74.5 us -> 71.2 us (0.956)
  Pallas kernels: 70.9 us -> 67.9 us
    pallas_call x1, Pallas kernels: 70.9 us -> 67.9 us  [body(): pl.pallas_call(functools.partial(kernel, nf, nq), out_shape=(jax.ShapeDty...]
    reshape x3 -> x0, local copies, waits for them, and re-layouts: 2.72 us -> none  [the longest x1 1.08 us: body(): orbitals.reshape(2, PLANES * HALF, LANES)]
    unnamed x10 -> x4, local copies, waits for them, and re-layouts: 0.03 us -> 2.52 us
where the time goes in v2:
time: 71.2 us; the launch traced here: 71.1 us
  Pallas kernels  67.9 us (95%)
  local copies, waits for them, and re-layouts  2.52 us (4%)
    pallas_call x1, Pallas kernels, body(): pl.pallas_call(functools.partial(kernel, nf, nq), out_shape=(jax.ShapeDty...  67.9 us
    unnamed x4, local copies, waits for them, and re-layouts  2.52 us

profile of v2, /device:TPU:1, one launch (start us, length us, event | category | flops | bytes accessed | tf_op | source)
XLA Modules:
  0.0 71.1 jit_solution(5606183843682778306)
XLA Ops:
  0.6 67.9 %shard_map.77 = (f32[2,8,4096]{2,1,0:T(8,128)}, f32[4,8,4096]{2,1,0:T(8,128)}) custom-call(f32[2,8,4096]{2,1,0:T(8,128)} %orb_hbm.1, bf16[256,256]{1,0:T(8,128)(2,1)} %constant.10.clone.fz_hbm, bf16[256,256]{1,0:T(8,128)(2,1)} %constant.11.clone.iz_hbm, bf16[128,256]{1,0:T(8,128)(2,1)} %constant.12.clone.fy_hbm, bf16[128,256]{1,0:T(8,128)(2,1)} %constant.13.clone.fx_hbm, ...), custom_call_target="tpu_custom_call" | custom-call | flops 1610612736 | bytes 1048576 | tf_op jit(solution)/shard_map/pallas_call | solution.py:425
  68.5 0.0 copy-start
  68.5 1.7 %copy.10 = f32[2,8,4096]{2,1,0:T(8,128)} copy(f32[2,8,4096]{2,1,0:T(8,128)} %get-tuple-element.4) | data formatting | bytes 524288
  70.3 0.0 copy-done
  70.3 0.8 %copy.11 = f32[4,8,4096]{2,1,0:T(8,128)} copy(f32[4,8,4096]{2,1,0:T(8,128)S(1)} %copy-done) | data formatting | bytes 1048576
Async XLA Ops:
  68.5 1.7 %copy-start = (f32[4,8,4096]{2,1,0:T(8,128)S(1)}, f32[4,8,4096]{2,1,0:T(8,128)}, u32[]{:S(2)}) copy-start(f32[4,8,4096]{2,1,0:T(8,128)} %get-tuple-element.5) | copy-start | bytes 1572868

commit v3 on v2

--- a/solution.py
+++ b/solution.py
@@ -94,9 +94,9 @@
     orb_hbm, fz_hbm, iz_hbm, fy_hbm, fx_hbm, iy_hbm,
     local_ref, window_ref,
     orb, fz, iz, fy, fx, iy,
-    obuf, dbuf, ktab, wbuf, fsend, frecv, bsend, brecv, part, pbuf, hbuf, rsbuf, acc, fin,
+    obuf, dbuf, ktab, wbuf, fsend, frecv, bsend, brecv, part, pbuf, hbuf, rsbuf, acc, fin, lbuf,
     in_sem, table_sem, sc_s, sc_r, ag_s, ag_r, cx_s, cx_r, f_s, f_r, b_s, b_r,
-    p_s, p_r, rs_s, rs_r, ga_s, ga_r, fx_s, fx_r,
+    p_s, p_r, rs_s, rs_r, ga_s, ga_r, fx_s, fx_r, out_sem,
 ):
     band = lax.axis_index("band")
     me = lax.axis_index("fft")
@@ -116,17 +116,16 @@
     def signal(b, f):
         pl.semaphore_signal(barrier, inc=1, device_id=(b, f), device_id_type=MESH)
 
+    @pl.when(jnp.logical_and(core == 0, chip != 0))
+    def _():
+        signal(0, me)
+
     @pl.when(jnp.logical_and(core == 1, chip != root_chip))
     def _():
         signal(second_root, me)
 
-    loop(1, nq, lambda step: signal(2 * lax.rem(chip + step, nq) + core, me))
     loop(1, nf, lambda step: signal(band, lax.rem(me + step, nf)))
     signal(other, me)
-
-    @pl.when(band == second_root)
-    def _():
-        loop(1, nq, lambda step: signal(2 * lax.rem(chip + step, nq) + 1, me))
 
     loads = [pltpu.make_async_copy(orb_hbm, orb, in_sem)]
     loads += [
@@ -139,10 +138,8 @@
         load.start()
     loads[0].wait()
 
-    extra = jnp.where(
-        band == second_root, nq - 1, jnp.where(jnp.logical_and(core == 1, chip != root_chip), 1, 0)
-    )
-    pl.semaphore_wait(barrier, nf - 1 + nq - 1 + 1 + extra)
+    extra = jnp.where(jnp.logical_or(band == 0, band == second_root), nq - 1, 0)
+    pl.semaphore_wait(barrier, nf - 1 + 1 + extra)
 
     def span(place):
         return pl.ds(pl.multiple_of(place * width, width), width)
@@ -333,30 +330,34 @@
         loop(1, nq, send)
 
     theirs = 2 - 2 * core
+    share = rows * LANES // PLANES
 
     def gather_sum(k):
         wait_for(rsbuf.at[k, pl.ds(0, nq - 1)], rs_r.at[k])
         total = rsbuf[k, 0]
         for slot in range(1, nq):
             total = total + rsbuf[k, slot]
-        fin[theirs + k, own_piece, :] = total
+        for index in range(rows // PLANES):
+            start = pl.multiple_of(chip * share + index * LANES, LANES)
+            fin[theirs + k, :, pl.ds(start, LANES)] = total[index * PLANES:(index + 1) * PLANES]
+        mine = fin.at[theirs + k, :, pl.ds(pl.multiple_of(chip * share, share), share)]
 
         def send(step):
             p = lax.rem(chip + step, nq)
             pltpu.make_async_remote_copy(
-                fin.at[theirs + k, own_piece, :], fin.at[theirs + k, own_piece, :],
+                mine, mine,
                 ga_s.at[k], ga_r.at[k], device_id=(2 * p + core, me), device_id_type=MESH,
             ).start()
 
         loop(1, nq, send)
 
+    def store(source, target, index):
+        pltpu.make_async_copy(source, target, out_sem.at[index]).start()
+
     def share_sum(k):
-        wait_for(fin.at[k, pl.ds(0, (nq - 1) * rows), :], ga_r.at[k])
+        wait_for(fin.at[k, :, pl.ds(0, (nq - 1) * share)], ga_r.at[k])
         to_partner(fin.at[theirs + k], fin.at[theirs + k], fx_s.at[k], fx_r.at[k])
-
-    def write_window(j, t):
-        start = pl.multiple_of(t * PLANES, PLANES)
-        window_ref[j, :, tile(t)] = fin[j, pl.ds(start, PLANES), :]
+        store(fin.at[theirs + k], window_ref.at[theirs + k], 1 + k)
 
     gather(0)
     gather(1)
@@ -378,14 +379,18 @@
     def unpack(t):
         even = acc[pl.ds(t, PLANES, stride=GRID), :]
         odd = acc[pl.ds(t + HALF, PLANES, stride=GRID), :]
-        local_ref[0, :, tile(t)] = jnp.where(tile_lane, even, pltpu.roll(odd, GRID, 1))
-        local_ref[1, :, tile(t)] = jnp.where(tile_lane, pltpu.roll(even, GRID, 1), odd)
+        lbuf[0, :, tile(t)] = jnp.where(tile_lane, even, pltpu.roll(odd, GRID, 1))
+        lbuf[1, :, tile(t)] = jnp.where(tile_lane, pltpu.roll(even, GRID, 1), odd)
 
     loop(0, HALF, unpack)
+    store(lbuf, local_ref, 0)
     for k in range(2):
         gather_sum(k)
     for k in range(2):
         share_sum(k)
+    for k in range(2):
+        wait_for(fin.at[k], fx_r.at[k])
+        store(fin.at[2 * core + k], window_ref.at[2 * core + k], 3 + k)
 
     @pl.when(band == 0)
     def _():
@@ -408,11 +413,11 @@
     for k in range(2):
         wait_for(pbuf.at[k], p_s.at[k])
         wait_for(rsbuf.at[k, pl.ds(0, nq - 1)], rs_s.at[k])
-        wait_for(fin.at[k, pl.ds(0, (nq - 1) * rows), :], ga_s.at[k])
+        wait_for(fin.at[k, :, pl.ds(0, (nq - 1) * share)], ga_s.at[k])
         wait_for(fin.at[k], fx_s.at[k])
-        wait_for(fin.at[k], fx_r.at[k])
-    for j in range(4):
-        loop(0, HALF, functools.partial(write_window, j))
+    wait_for(lbuf, out_sem.at[0])
+    for index in range(4):
+        wait_for(fin.at[index], out_sem.at[1 + index])
 
 
 def body(orbitals):
@@ -429,7 +434,7 @@
             jax.ShapeDtypeStruct((4, PLANES, GRID * GRID), F32),
         ),
         in_specs=[pl.BlockSpec(memory_space=pltpu.HBM)] * 6,
-        out_specs=(pl.BlockSpec(memory_space=vmem),) * 2,
+        out_specs=(pl.BlockSpec(memory_space=pltpu.HBM),) * 2,
         scratch_shapes=[
             vmem((2, PLANES, GRID * GRID), F32),
             vmem((256, 256), BF16),
@@ -450,11 +455,12 @@
             vmem((2, 256, LANES), F32),
             vmem((2, nq, rows, LANES), F32),
             vmem((PLANES * GRID, LANES), F32),
-            vmem((4, 256, LANES), F32),
+            vmem((4, PLANES, GRID * GRID), F32),
+            vmem((2, PLANES, GRID * GRID), F32),
             dma, dma((5,)), dma((2,)), dma((2,)), dma((2,)), dma((2,)), dma((2,)), dma((2,)),
             dma((4,)), dma((4,)), dma((4,)), dma((4,)),
             dma((2,)), dma((2,)), dma((2,)), dma((2,)),
-            dma((2,)), dma((2,)), dma((2,)), dma((2,)),
+            dma((2,)), dma((2,)), dma((2,)), dma((2,)), dma((5,)),
         ],
         compiler_params=pltpu.CompilerParams(
             collective_id=0, has_side_effects=True, vmem_limit_bytes=56 * 1024 * 1024

time: 71.2 us -> 70.3 us (0.987)
  Pallas kernels: 67.9 us -> 67.1 us
    pallas_call x1, Pallas kernels: 67.9 us -> 67.1 us  [body(): pl.pallas_call(functools.partial(kernel, nf, nq), out_shape=(jax.ShapeDty...]
where the time goes in v3:
time: 70.3 us; the launch traced here: 70.2 us
  Pallas kernels  67.1 us (95%)
  local copies, waits for them, and re-layouts  2.52 us (4%)
    pallas_call x1, Pallas kernels, body(): pl.pallas_call(functools.partial(kernel, nf, nq), out_shape=(jax.ShapeDty...  67.1 us
    unnamed x4, local copies, waits for them, and re-layouts  2.52 us

profile of v3, /device:TPU:1, one launch (start us, length us, event | category | flops | bytes accessed | tf_op | source)
XLA Modules:
  0.0 70.2 jit_solution(4706870383723224338)
XLA Ops:
  0.6 67.1 %shard_map.77 = (f32[2,8,4096]{2,1,0:T(8,128)}, f32[4,8,4096]{2,1,0:T(8,128)}) custom-call(f32[2,8,4096]{2,1,0:T(8,128)} %orb_hbm.1, bf16[256,256]{1,0:T(8,128)(2,1)} %constant.10.clone.fz_hbm, bf16[256,256]{1,0:T(8,128)(2,1)} %constant.11.clone.iz_hbm, bf16[128,256]{1,0:T(8,128)(2,1)} %constant.12.clone.fy_hbm, bf16[128,256]{1,0:T(8,128)(2,1)} %constant.13.clone.fx_hbm, ...), custom_call_target="tpu_custom_call" | custom-call | flops 1610612736 | bytes 1048576 | tf_op jit(solution)/shard_map/pallas_call | solution.py:430
  67.7 0.0 copy-start
  67.7 1.7 %copy.10 = f32[2,8,4096]{2,1,0:T(8,128)} copy(f32[2,8,4096]{2,1,0:T(8,128)} %get-tuple-element.4) | data formatting | bytes 524288
  69.4 0.0 copy-done
  69.4 0.8 %copy.11 = f32[4,8,4096]{2,1,0:T(8,128)} copy(f32[4,8,4096]{2,1,0:T(8,128)S(1)} %copy-done) | data formatting | bytes 1048576
Async XLA Ops:
  67.7 1.7 %copy-start = (f32[4,8,4096]{2,1,0:T(8,128)S(1)}, f32[4,8,4096]{2,1,0:T(8,128)}, u32[]{:S(2)}) copy-start(f32[4,8,4096]{2,1,0:T(8,128)} %get-tuple-element.5) | copy-start | bytes 1572868

commit v4 on v3

--- a/solution.py
+++ b/solution.py
@@ -83,6 +83,11 @@
         return carry
 
     lax.fori_loop(first, last, advance, 0, unroll=last - first)
+
+
+def far_first(count, step):
+    half = count // 2
+    loop(0, count - 1, lambda i: step(half + (1 - 2 * lax.rem(i, 2)) * ((i + 1) // 2)))
 
 
 def wait_for(ref, sem):
@@ -159,12 +164,13 @@
                 orb.at[window, :, pl.ds(0, width)], wbuf.at[window, :, pl.ds(0, width)],
                 sc_r.at[window],
             ).start()
-            loop(1, nq, lambda p: scatter(window, 0, p))
+            far_first(nq, lambda step: scatter(window, 0, step))
 
     @pl.when(band == second_root)
     def _():
         for window in range(2):
-            loop(0, nq, lambda p: scatter(window, 1, p))
+            far_first(nq, lambda step: scatter(window, 1, lax.rem(chip + step, nq)))
+            scatter(window, 1, chip)
 
     lane = lax.broadcasted_iota(jnp.int32, (GRID, LANES), 1)
     low_lane = lane < GRID
@@ -216,7 +222,7 @@
                 device_id=(2 * p + core, me), device_id_type=MESH,
             ).start()
 
-        loop(1, levels, send)
+        far_first(levels, send)
 
     def cross(window):
         wait_for(wbuf.at[window, :, pl.ds(0, (levels - 1) * width)], ag_r.at[window])
@@ -327,7 +333,7 @@
                 rs_s.at[k], rs_r.at[k], device_id=(2 * p + core, me), device_id_type=MESH,
             ).start()
 
-        loop(1, nq, send)
+        far_first(nq, send)
 
     theirs = 2 - 2 * core
     share = rows * LANES // PLANES
@@ -349,7 +355,7 @@
                 ga_s.at[k], ga_r.at[k], device_id=(2 * p + core, me), device_id_type=MESH,
             ).start()
 
-        loop(1, nq, send)
+        far_first(nq, send)
 
     def store(source, target, index):
         pltpu.make_async_copy(source, target, out_sem.at[index]).start()
@@ -463,12 +469,12 @@
             dma((2,)), dma((2,)), dma((2,)), dma((2,)), dma((5,)),
         ],
         compiler_params=pltpu.CompilerParams(
-            collective_id=0, has_side_effects=True, vmem_limit_bytes=56 * 1024 * 1024
+            collective_id=0, has_side_effects=True, vmem_limit_bytes=40 * 1024 * 1024
         ),
         cost_estimate=pl.CostEstimate(
             flops=6 * 4 * 2 * 512 * 256 * 256, bytes_accessed=1 << 20, transcendentals=0
         ),
-    )(orbitals, *tables)
+    )(*[pltpu.with_memory_space_constraint(a, pltpu.HBM) for a in (orbitals, *tables)])
     return local_out, window_out
 
 

time: 70.3 us -> 66.6 us (0.947)
  Pallas kernels: 67.1 us -> 64.4 us
  local copies, waits for them, and re-layouts: 2.52 us -> 1.5 us
    pallas_call x1, Pallas kernels: 67.1 us -> 64.4 us  [body(): pl.pallas_call(functools.partial(kernel, nf, nq), out_shape=(jax.ShapeDty...]
    unnamed x4 -> x2, local copies, waits for them, and re-layouts: 2.52 us -> 1.5 us
where the time goes in v4:
time: 66.6 us; the launch traced here: 66.5 us
  Pallas kernels  64.4 us (97%)
  local copies, waits for them, and re-layouts  1.5 us (2%)
    pallas_call x1, Pallas kernels, body(): pl.pallas_call(functools.partial(kernel, nf, nq), out_shape=(jax.ShapeDty...  64.4 us
    unnamed x2, local copies, waits for them, and re-layouts  1.5 us

profile of v4, /device:TPU:1, one launch (start us, length us, event | category | flops | bytes accessed | tf_op | source)
XLA Modules:
  0.0 66.5 jit_solution(9217553548052275894)
XLA Ops:
  0.6 64.4 %shard_map.77 = (f32[2,8,4096]{2,1,0:T(8,128)S(1)}, f32[4,8,4096]{2,1,0:T(8,128)S(1)}) custom-call(f32[2,8,4096]{2,1,0:T(8,128)} %orb_hbm.1, bf16[256,256]{1,0:T(8,128)(2,1)} %constant.10.clone.fz_hbm, bf16[256,256]{1,0:T(8,128)(2,1)} %constant.11.clone.iz_hbm, bf16[128,256]{1,0:T(8,128)(2,1)} %constant.12.clone.fy_hbm, ...), custom_call_target="tpu_custom_call" | custom-call | flops 1610612736 | bytes 1048576 | tf_op jit(solution)/shard_map/pallas_call | solution.py:436
  65.0 0.7 %copy.10 = f32[2,8,4096]{2,1,0:T(8,128)} copy(f32[2,8,4096]{2,1,0:T(8,128)S(1)} %get-tuple-element.4) | data formatting | bytes 524288
  65.7 0.8 %copy.11 = f32[4,8,4096]{2,1,0:T(8,128)} copy(f32[4,8,4096]{2,1,0:T(8,128)S(1)} %get-tuple-element.5) | data formatting | bytes 1048576

commit v5 on v4

--- a/solution.py
+++ b/solution.py
@@ -88,6 +88,16 @@
 def far_first(count, step):
     half = count // 2
     loop(0, count - 1, lambda i: step(half + (1 - 2 * lax.rem(i, 2)) * ((i + 1) // 2)))
+
+
+def pairs_far_first(count, step):
+    half = count // 2
+
+    def both(i):
+        k = i // 2
+        step(half + (1 - 2 * lax.rem(k, 2)) * ((k + 1) // 2), 1 - lax.rem(i, 2))
+
+    loop(0, 2 * count - 1, both)
 
 
 def wait_for(ref, sem):
@@ -116,6 +126,10 @@
     level, column = chip // columns, lax.rem(chip, columns)
     width = GRID * GRID // levels
 
+    def chip_at(up, across):
+        return lax.rem(level + up, levels) * columns + lax.rem(column + across, columns)
+
+
     barrier = pltpu.get_barrier_semaphore()
 
     def signal(b, f):
@@ -164,12 +178,12 @@
                 orb.at[window, :, pl.ds(0, width)], wbuf.at[window, :, pl.ds(0, width)],
                 sc_r.at[window],
             ).start()
-            far_first(nq, lambda step: scatter(window, 0, step))
+            pairs_far_first(levels, lambda up, across: scatter(window, 0, chip_at(up, across)))
 
     @pl.when(band == second_root)
     def _():
         for window in range(2):
-            far_first(nq, lambda step: scatter(window, 1, lax.rem(chip + step, nq)))
+            pairs_far_first(levels, lambda up, across: scatter(window, 1, chip_at(up, across)))
             scatter(window, 1, chip)
 
     lane = lax.broadcasted_iota(jnp.int32, (GRID, LANES), 1)
@@ -326,14 +340,14 @@
         hbuf[k] = part[k + 2] + pbuf[k]
         rsbuf[k, chip] = hbuf[k, own_piece, :]
 
-        def send(step):
-            p = lax.rem(chip + step, nq)
+        def send(up, across):
+            p = chip_at(up, across)
             pltpu.make_async_remote_copy(
                 hbuf.at[k, pl.ds(pl.multiple_of(p * rows, rows), rows), :], rsbuf.at[k, chip],
                 rs_s.at[k], rs_r.at[k], device_id=(2 * p + core, me), device_id_type=MESH,
             ).start()
 
-        far_first(nq, send)
+        pairs_far_first(levels, send)
 
     theirs = 2 - 2 * core
     share = rows * LANES // PLANES
@@ -348,14 +362,14 @@
             fin[theirs + k, :, pl.ds(start, LANES)] = total[index * PLANES:(index + 1) * PLANES]
         mine = fin.at[theirs + k, :, pl.ds(pl.multiple_of(chip * share, share), share)]
 
-        def send(step):
-            p = lax.rem(chip + step, nq)
+        def send(up, across):
+            p = chip_at(up, across)
             pltpu.make_async_remote_copy(
                 mine, mine,
                 ga_s.at[k], ga_r.at[k], device_id=(2 * p + core, me), device_id_type=MESH,
             ).start()
 
-        far_first(nq, send)
+        pairs_far_first(levels, send)
 
     def store(source, target, index):
         pltpu.make_async_copy(source, target, out_sem.at[index]).start()

time: 66.6 us -> 66.2 us (level)
  no operation moved by 1% of the time
where the time goes in v5:
time: 66.2 us; the launch traced here: 66.1 us
  Pallas kernels  64 us (97%)
  local copies, waits for them, and re-layouts  1.5 us (2%)
    pallas_call x1, Pallas kernels, body(): pl.pallas_call(functools.partial(kernel, nf, nq), out_shape=(jax.ShapeDty...  64 us
    unnamed x2, local copies, waits for them, and re-layouts  1.5 us

profile of v5, /device:TPU:1, one launch (start us, length us, event | category | flops | bytes accessed | tf_op | source)
XLA Modules:
  0.0 66.1 jit_solution(11882305846591543595)
XLA Ops:
  0.6 64.0 %shard_map.77 = (f32[2,8,4096]{2,1,0:T(8,128)S(1)}, f32[4,8,4096]{2,1,0:T(8,128)S(1)}) custom-call(f32[2,8,4096]{2,1,0:T(8,128)} %orb_hbm.1, bf16[256,256]{1,0:T(8,128)(2,1)} %constant.10.clone.fz_hbm, bf16[256,256]{1,0:T(8,128)(2,1)} %constant.11.clone.iz_hbm, bf16[128,256]{1,0:T(8,128)(2,1)} %constant.12.clone.fy_hbm, ...), custom_call_target="tpu_custom_call" | custom-call | flops 1610612736 | bytes 1048576 | tf_op jit(solution)/shard_map/pallas_call | solution.py:450
  64.6 0.7 %copy.10 = f32[2,8,4096]{2,1,0:T(8,128)} copy(f32[2,8,4096]{2,1,0:T(8,128)S(1)} %get-tuple-element.4) | data formatting | bytes 524288
  65.3 0.8 %copy.11 = f32[4,8,4096]{2,1,0:T(8,128)} copy(f32[4,8,4096]{2,1,0:T(8,128)S(1)} %get-tuple-element.5) | data formatting | bytes 1048576

commit v6 on v5

--- a/solution.py
+++ b/solution.py
@@ -109,9 +109,9 @@
     orb_hbm, fz_hbm, iz_hbm, fy_hbm, fx_hbm, iy_hbm,
     local_ref, window_ref,
     orb, fz, iz, fy, fx, iy,
-    obuf, dbuf, ktab, wbuf, fsend, frecv, bsend, brecv, part, pbuf, hbuf, rsbuf, acc, fin, lbuf,
+    obuf, dbuf, ktab, wbuf, fsend, frecv, bsend, brecv, part, pbuf, hbuf, rsbuf, acc,
     in_sem, table_sem, sc_s, sc_r, ag_s, ag_r, cx_s, cx_r, f_s, f_r, b_s, b_r,
-    p_s, p_r, rs_s, rs_r, ga_s, ga_r, fx_s, fx_r, out_sem,
+    p_s, p_r, rs_s, rs_r, ga_s, ga_r, fx_s, fx_r,
 ):
     band = lax.axis_index("band")
     me = lax.axis_index("fft")
@@ -249,6 +249,8 @@
     block = GRID * PLANES // nf
 
     def exchange(source, target, send_sem, recv_sem, k):
+        if k >= 2:
+            wait_for(target.at[k - 2, pl.ds(0, nf - 1)], send_sem.at[k - 2])
         own = pl.ds(pl.multiple_of(me * block, block), block)
         pltpu.make_async_copy(source.at[k, own, :], target.at[k, me], recv_sem.at[k]).start()
 
@@ -263,7 +265,7 @@
         loop(1, nf, send)
 
     def forward(k):
-        j = lax.rem(2 * core + k, 4)
+        j = (2 * core if k % 2 == 0 else 2 - 2 * core) + k // 2
 
         def widen(t):
             values = wbuf[j, :, tile(t)]
@@ -337,7 +339,7 @@
 
     def scatter_sum(k):
         wait_for(pbuf.at[k], p_r.at[k])
-        hbuf[k] = part[k + 2] + pbuf[k]
+        hbuf[k] = part[2 * k + 1] + pbuf[k]
         rsbuf[k, chip] = hbuf[k, own_piece, :]
 
         def send(up, across):
@@ -359,8 +361,8 @@
             total = total + rsbuf[k, slot]
         for index in range(rows // PLANES):
             start = pl.multiple_of(chip * share + index * LANES, LANES)
-            fin[theirs + k, :, pl.ds(start, LANES)] = total[index * PLANES:(index + 1) * PLANES]
-        mine = fin.at[theirs + k, :, pl.ds(pl.multiple_of(chip * share, share), share)]
+            window_ref[theirs + k, :, pl.ds(start, LANES)] = total[index * PLANES:(index + 1) * PLANES]
+        mine = window_ref.at[theirs + k, :, pl.ds(pl.multiple_of(chip * share, share), share)]
 
         def send(up, across):
             p = chip_at(up, across)
@@ -371,46 +373,40 @@
 
         pairs_far_first(levels, send)
 
-    def store(source, target, index):
-        pltpu.make_async_copy(source, target, out_sem.at[index]).start()
-
     def share_sum(k):
-        wait_for(fin.at[k, :, pl.ds(0, (nq - 1) * share)], ga_r.at[k])
-        to_partner(fin.at[theirs + k], fin.at[theirs + k], fx_s.at[k], fx_r.at[k])
-        store(fin.at[theirs + k], window_ref.at[theirs + k], 1 + k)
+        wait_for(window_ref.at[k, :, pl.ds(0, (nq - 1) * share)], ga_r.at[k])
+        to_partner(window_ref.at[theirs + k], window_ref.at[theirs + k], fx_s.at[k], fx_r.at[k])
 
     gather(0)
     gather(1)
     for window in range(2):
         cross(window)
-        forward(window)
-    for window in range(2):
+        forward(2 * window)
         wait_for(wbuf.at[window], cx_r.at[window])
-        forward(window + 2)
-    for k in range(4):
+        if window == 1:
+            middle(0)
+        forward(2 * window + 1)
+    for k in range(1, 4):
         middle(k)
     for k in range(2):
-        backward(k)
-        to_partner(part.at[k], pbuf.at[k], p_s.at[k], p_r.at[k])
-    for k in range(2):
-        backward(k + 2)
+        backward(2 * k)
+        to_partner(part.at[2 * k], pbuf.at[k], p_s.at[k], p_r.at[k])
+        backward(2 * k + 1)
         scatter_sum(k)
 
     def unpack(t):
         even = acc[pl.ds(t, PLANES, stride=GRID), :]
         odd = acc[pl.ds(t + HALF, PLANES, stride=GRID), :]
-        lbuf[0, :, tile(t)] = jnp.where(tile_lane, even, pltpu.roll(odd, GRID, 1))
-        lbuf[1, :, tile(t)] = jnp.where(tile_lane, pltpu.roll(even, GRID, 1), odd)
+        local_ref[0, :, tile(t)] = jnp.where(tile_lane, even, pltpu.roll(odd, GRID, 1))
+        local_ref[1, :, tile(t)] = jnp.where(tile_lane, pltpu.roll(even, GRID, 1), odd)
 
     loop(0, HALF, unpack)
-    store(lbuf, local_ref, 0)
     for k in range(2):
         gather_sum(k)
     for k in range(2):
         share_sum(k)
     for k in range(2):
-        wait_for(fin.at[k], fx_r.at[k])
-        store(fin.at[2 * core + k], window_ref.at[2 * core + k], 3 + k)
+        wait_for(window_ref.at[k], fx_r.at[k])
 
     @pl.when(band == 0)
     def _():
@@ -427,17 +423,14 @@
     for window in range(2):
         wait_for(wbuf.at[window, :, pl.ds(0, (levels - 1) * width)], ag_s.at[window])
         wait_for(wbuf.at[window], cx_s.at[window])
-    for k in range(4):
+    for k in range(2, 4):
         wait_for(frecv.at[k, pl.ds(0, nf - 1)], f_s.at[k])
         wait_for(brecv.at[k, pl.ds(0, nf - 1)], b_s.at[k])
     for k in range(2):
         wait_for(pbuf.at[k], p_s.at[k])
         wait_for(rsbuf.at[k, pl.ds(0, nq - 1)], rs_s.at[k])
-        wait_for(fin.at[k, :, pl.ds(0, (nq - 1) * share)], ga_s.at[k])
-        wait_for(fin.at[k], fx_s.at[k])
-    wait_for(lbuf, out_sem.at[0])
-    for index in range(4):
-        wait_for(fin.at[index], out_sem.at[1 + index])
+        wait_for(window_ref.at[k, :, pl.ds(0, (nq - 1) * share)], ga_s.at[k])
+        wait_for(window_ref.at[k], fx_s.at[k])
 
 
 def body(orbitals):
@@ -454,7 +447,7 @@
             jax.ShapeDtypeStruct((4, PLANES, GRID * GRID), F32),
         ),
         in_specs=[pl.BlockSpec(memory_space=pltpu.HBM)] * 6,
-        out_specs=(pl.BlockSpec(memory_space=pltpu.HBM),) * 2,
+        out_specs=(pl.BlockSpec(memory_space=vmem),) * 2,
         scratch_shapes=[
             vmem((2, PLANES, GRID * GRID), F32),
             vmem((256, 256), BF16),
@@ -475,12 +468,10 @@
             vmem((2, 256, LANES), F32),
             vmem((2, nq, rows, LANES), F32),
             vmem((PLANES * GRID, LANES), F32),
-            vmem((4, PLANES, GRID * GRID), F32),
-            vmem((2, PLANES, GRID * GRID), F32),
             dma, dma((5,)), dma((2,)), dma((2,)), dma((2,)), dma((2,)), dma((2,)), dma((2,)),
             dma((4,)), dma((4,)), dma((4,)), dma((4,)),
             dma((2,)), dma((2,)), dma((2,)), dma((2,)),
-            dma((2,)), dma((2,)), dma((2,)), dma((2,)), dma((5,)),
+            dma((2,)), dma((2,)), dma((2,)), dma((2,)),
         ],
         compiler_params=pltpu.CompilerParams(
             collective_id=0, has_side_effects=True, vmem_limit_bytes=40 * 1024 * 1024

time: 66.2 us -> 65.4 us (0.988)
  Pallas kernels: 64 us -> 63.1 us
    pallas_call x1, Pallas kernels: 64 us -> 63.1 us  [body(): pl.pallas_call(functools.partial(kernel, nf, nq), out_shape=(jax.ShapeDty...]
where the time goes in v6:
time: 65.4 us; the launch traced here: 65.3 us
  Pallas kernels  63.1 us (96%)
  local copies, waits for them, and re-layouts  1.5 us (2%)
    pallas_call x1, Pallas kernels, body(): pl.pallas_call(functools.partial(kernel, nf, nq), out_shape=(jax.ShapeDty...  63.1 us
    unnamed x2, local copies, waits for them, and re-layouts  1.5 us

profile of v6, /device:TPU:1, one launch (start us, length us, event | category | flops | bytes accessed | tf_op | source)
XLA Modules:
  0.0 65.3 jit_solution(13322056052166051424)
XLA Ops:
  0.6 63.1 %shard_map.77 = (f32[2,8,4096]{2,1,0:T(8,128)S(1)}, f32[4,8,4096]{2,1,0:T(8,128)S(1)}) custom-call(f32[2,8,4096]{2,1,0:T(8,128)} %orb_hbm.1, bf16[256,256]{1,0:T(8,128)(2,1)} %constant.10.clone.fz_hbm, bf16[256,256]{1,0:T(8,128)(2,1)} %constant.11.clone.iz_hbm, bf16[128,256]{1,0:T(8,128)(2,1)} %constant.12.clone.fy_hbm, ...), custom_call_target="tpu_custom_call" | custom-call | flops 1610612736 | bytes 1048576 | tf_op jit(solution)/shard_map/pallas_call | solution.py:443
  63.8 0.7 %copy.10 = f32[2,8,4096]{2,1,0:T(8,128)} copy(f32[2,8,4096]{2,1,0:T(8,128)S(1)} %get-tuple-element.4) | data formatting | bytes 524288
  64.5 0.8 %copy.11 = f32[4,8,4096]{2,1,0:T(8,128)} copy(f32[4,8,4096]{2,1,0:T(8,128)S(1)} %get-tuple-element.5) | data formatting | bytes 1048576

commit v7 on v6

--- a/solution.py
+++ b/solution.py
@@ -378,9 +378,10 @@
         to_partner(window_ref.at[theirs + k], window_ref.at[theirs + k], fx_s.at[k], fx_r.at[k])
 
     gather(0)
-    gather(1)
     for window in range(2):
         cross(window)
+        if window == 0:
+            gather(1)
         forward(2 * window)
         wait_for(wbuf.at[window], cx_r.at[window])
         if window == 1:

time: 65.4 us -> 65 us (level)
  no operation moved by 1% of the time
where the time goes in v7:
time: 65 us; the launch traced here: 64.9 us
  Pallas kernels  62.8 us (97%)
  local copies, waits for them, and re-layouts  1.5 us (2%)
    pallas_call x1, Pallas kernels, body(): pl.pallas_call(functools.partial(kernel, nf, nq), out_shape=(jax.ShapeDty...  62.8 us
    unnamed x2, local copies, waits for them, and re-layouts  1.5 us

profile of v7, /device:TPU:1, one launch (start us, length us, event | category | flops | bytes accessed | tf_op | source)
XLA Modules:
  0.0 64.9 jit_solution(3993837977491937384)
XLA Ops:
  0.6 62.8 %shard_map.77 = (f32[2,8,4096]{2,1,0:T(8,128)S(1)}, f32[4,8,4096]{2,1,0:T(8,128)S(1)}) custom-call(f32[2,8,4096]{2,1,0:T(8,128)} %orb_hbm.1, bf16[256,256]{1,0:T(8,128)(2,1)} %constant.10.clone.fz_hbm, bf16[256,256]{1,0:T(8,128)(2,1)} %constant.11.clone.iz_hbm, bf16[128,256]{1,0:T(8,128)(2,1)} %constant.12.clone.fy_hbm, ...), custom_call_target="tpu_custom_call" | custom-call | flops 1610612736 | bytes 1048576 | tf_op jit(solution)/shard_map/pallas_call | solution.py:444
  63.4 0.7 %copy.10 = f32[2,8,4096]{2,1,0:T(8,128)} copy(f32[2,8,4096]{2,1,0:T(8,128)S(1)} %get-tuple-element.4) | data formatting | bytes 524288
  64.1 0.8 %copy.11 = f32[4,8,4096]{2,1,0:T(8,128)} copy(f32[4,8,4096]{2,1,0:T(8,128)S(1)} %get-tuple-element.5) | data formatting | bytes 1048576

commit v8 on v7

--- a/solution.py
+++ b/solution.py
@@ -252,17 +252,17 @@
         if k >= 2:
             wait_for(target.at[k - 2, pl.ds(0, nf - 1)], send_sem.at[k - 2])
         own = pl.ds(pl.multiple_of(me * block, block), block)
-        pltpu.make_async_copy(source.at[k, own, :], target.at[k, me], recv_sem.at[k]).start()
-
-        def send(step):
-            p = lax.rem(me + step, nf)
+
+        def send(up, across):
+            p = lax.rem(me // 4 + across, 2) * 4 + lax.rem(lax.rem(me, 4) + up, 4)
             pltpu.make_async_remote_copy(
                 source.at[k, pl.ds(pl.multiple_of(p * block, block), block), :],
                 target.at[k, me], send_sem.at[k], recv_sem.at[k],
                 device_id=(band, p), device_id_type=MESH,
             ).start()
 
-        loop(1, nf, send)
+        pairs_far_first(4, send)
+        pltpu.make_async_copy(source.at[k, own, :], target.at[k, me], recv_sem.at[k]).start()
 
     def forward(k):
         j = (2 * core if k % 2 == 0 else 2 - 2 * core) + k // 2

time: 65 us -> 65.1 us (level)
  no operation moved by 1% of the time
where the time goes in v8:
time: 65.1 us; the launch traced here: 65 us
  Pallas kernels  62.8 us (96%)
  local copies, waits for them, and re-layouts  1.5 us (2%)
    pallas_call x1, Pallas kernels, body(): pl.pallas_call(functools.partial(kernel, nf, nq), out_shape=(jax.ShapeDty...  62.8 us
    unnamed x2, local copies, waits for them, and re-layouts  1.5 us

profile of v8, /device:TPU:1, one launch (start us, length us, event | category | flops | bytes accessed | tf_op | source)
XLA Modules:
  0.0 65.0 jit_solution(18151131037890593965)
XLA Ops:
  0.6 62.8 %shard_map.77 = (f32[2,8,4096]{2,1,0:T(8,128)S(1)}, f32[4,8,4096]{2,1,0:T(8,128)S(1)}) custom-call(f32[2,8,4096]{2,1,0:T(8,128)} %orb_hbm.1, bf16[256,256]{1,0:T(8,128)(2,1)} %constant.10.clone.fz_hbm, bf16[256,256]{1,0:T(8,128)(2,1)} %constant.11.clone.iz_hbm, bf16[128,256]{1,0:T(8,128)(2,1)} %constant.12.clone.fy_hbm, ...), custom_call_target="tpu_custom_call" | custom-call | flops 1610612736 | bytes 1048576 | tf_op jit(solution)/shard_map/pallas_call | solution.py:444
  63.5 0.7 %copy.10 = f32[2,8,4096]{2,1,0:T(8,128)} copy(f32[2,8,4096]{2,1,0:T(8,128)S(1)} %get-tuple-element.4) | data formatting | bytes 524288
  64.2 0.8 %copy.11 = f32[4,8,4096]{2,1,0:T(8,128)} copy(f32[4,8,4096]{2,1,0:T(8,128)S(1)} %get-tuple-element.5) | data formatting | bytes 1048576
